TPU v7x, 512 devices: a whole 4x8x8 slice. The times are simulated.
512 devices in a mesh: ia: 8 (over y), ja: 8 (over z_lo, x), al: 8 (over z_hi, core).
Axes of the slice: x: 4, y: 8, z: 8 (z_hi: 4, z_lo: 2; z = z_hi * 2 + z_lo), core: 2. Of those that a mesh axis runs over, the one named last changes fastest.
Arguments:
- inputs: bfloat16 [12288, 1024], P(('ia', 'ja'), 'al'), may hold values from -6 to 6
- out_grad: bfloat16 [12288, 1024], P(('ia', 'ja'), 'al'), may hold values from -6 to 6
- pre_act: bfloat16 [24576, 1024], P(('ja', 'ia'), 'al'), may hold values from -8 to 8
- w_up: bfloat16 [12288, 24576], P(('ia', 'al'), 'ja'), may hold values from -0.0390625 to 0.0390625
- w_down: bfloat16 [12288, 24576], P(('ia', 'al'), 'ja'), may hold values from -0.0546875 to 0.0546875
Outputs:
- input_grad: bfloat16 [12288, 1024], P(('ia', 'ja'), 'al')
- up_grad: bfloat16 [12288, 24576], P(('ia', 'al'), 'ja')
- down_grad: bfloat16 [12288, 24576], P(('ia', 'al'), 'ja')
All inputs are finite; a program needn't handle non-finite values.
Results may differ from a plain program's by a relative error of at most 0.025.
Values may be sent and summed in bfloat16 or wider, within the bound.
A program may use at most 128 MiB of HBM per device.

v0:
```python
import math

import jax
import jax.numpy as jnp
from jax import lax
from jax.sharding import PartitionSpec as P

gelu_root = math.sqrt(2.0 / math.pi)
gelu_cubic = 0.044715


def gelu_parts(pre):
    value = pre.astype(jnp.float32)
    tangent = jnp.tanh(gelu_root * (value + gelu_cubic * value * value * value))
    active = 0.5 * value * (1.0 + tangent)
    slope = 0.5 * (1.0 + tangent) + 0.5 * value * (1.0 - tangent * tangent) * gelu_root * (
        1.0 + 3.0 * gelu_cubic * value * value
    )
    return (active, slope)


def contract_last(left, right):
    return lax.dot_general(
        left, right, (((1,), (1,)), ((), ())), preferred_element_type=jnp.float32
    )


def contract_first(left, right):
    return lax.dot_general(
        left, right, (((0,), (0,)), ((), ())), preferred_element_type=jnp.float32
    )


def rounded(value):
    return lax.optimization_barrier(value.astype(jnp.bfloat16)).astype(jnp.float32)


def token_block_sum(row_mat, col_mat, depth_count, row_count, grad_scale):
    feature_rows = row_mat.shape[0]
    tile_rows = math.gcd(feature_rows, 256)
    tile_count = feature_rows // tile_rows
    row_tiles = row_mat.reshape(tile_count, tile_rows, row_mat.shape[1])

    def one_tile(tile):

        def one_add_block(level, total):
            start = (level * row_count).astype(jnp.int32)
            left = lax.dynamic_slice_in_dim(tile, start, row_count, 1)
            right = lax.dynamic_slice_in_dim(col_mat, start, row_count, 1)
            return total + rounded(contract_last(left, right) * grad_scale)

        blank = jnp.zeros((tile_rows, col_mat.shape[0]), jnp.float32)
        total = lax.fori_loop(0, depth_count, one_add_block, blank)
        return total.astype(jnp.bfloat16)

    tiles = lax.map(one_tile, row_tiles)
    return tiles.reshape(feature_rows, col_mat.shape[0])


def shards(inputs, out_grad, pre_act, w_up, w_down):
    tokens_full, grads_full = (
        lax.all_gather(inputs, "ja", axis=0, tiled=True),
        lax.all_gather(out_grad, "ja", axis=0, tiled=True),
    )
    row_count = inputs.shape[1]
    depth_count = lax.axis_size("al")
    grad_scale = float(row_count * depth_count) ** (-0.5)
    pre_full = lax.all_gather(pre_act, "ia", axis=0, tiled=True)
    act_partial = contract_first(lax.all_gather(w_down, "al", axis=0, tiled=True), grads_full)
    act_grad = lax.psum(act_partial.astype(jnp.bfloat16), "ia").astype(jnp.float32)
    active, slope = gelu_parts(pre_full)
    act_full = active.astype(jnp.bfloat16)
    hidden_grad = (act_grad * slope).astype(jnp.bfloat16)
    input_terms = jnp.dot(
        lax.all_gather(w_up, "al", axis=0, tiled=True),
        hidden_grad,
        preferred_element_type=jnp.float32,
    )
    input_grad = lax.psum_scatter(
        input_terms.astype(jnp.bfloat16), "ja", scatter_dimension=0, tiled=True
    )
    token_rows, grad_rows = (
        lax.all_to_all(tokens_full, "al", split_axis=0, concat_axis=1, tiled=True),
        lax.all_to_all(grads_full, "al", split_axis=0, concat_axis=1, tiled=True),
    )
    act_cols, hidden_cols = (
        lax.all_gather(act_full, "al", axis=1, tiled=True),
        lax.all_gather(hidden_grad, "al", axis=1, tiled=True),
    )
    up_grad = token_block_sum(token_rows, hidden_cols, depth_count, row_count, grad_scale)
    down_grad = token_block_sum(grad_rows, act_cols, depth_count, row_count, grad_scale)
    return (input_grad, up_grad, down_grad)


def solution(mesh):
    in_specs = (
        P(("ia", "ja"), "al"),
        P(("ia", "ja"), "al"),
        P(("ja", "ia"), "al"),
        P(("ia", "al"), "ja"),
        P(("ia", "al"), "ja"),
    )
    out_specs = (P(("ia", "ja"), "al"), P(("ia", "al"), "ja"), P(("ia", "al"), "ja"))
    return jax.shard_map(shards, mesh=mesh, in_specs=in_specs, out_specs=out_specs, check_vma=False)
```

profile of v0, /device:TPU:1, one launch (start us, length us, event | category | flops | bytes accessed | tf_op | source)
XLA Modules:
  0.0 531.9 jit_solution(648298996738068315)
XLA Ops:
  7.9 27.0 %all_gather.22 = bf16[1536,128]{1,0:T(8,128)(2,1)} all-gather(bf16[192,128]{1,0:T(8,128)(2,1)} %param.14), channel_id=1, replica_groups=mesh['ia'=8,'ja'=8,'al'=8] {'ja'}, dimensions={0}, use_global_device_ids=true | all-gather | bytes 442368 | tf_op jit(solution)/shard_map/all_gather | solution.py:63
  35.0 82.8 %all-gather.5.cloned.1.call-done = bf16[1536,3072]{1,0:T(8,128)(2,1)} async-done(((bf16[192,3072]{1,0:T(8,128)(2,1)}), bf16[1536,3072]{1,0:T(8,128)(2,1)}) %all-gather.5.cloned.1.call-update) | async-done | bytes 9437200 | tf_op jit(solution)/shard_map/all_gather | solution.py:69
  117.8 7.2 %convolution_convert_fusion = bf16[3072,128]{1,0:T(8,128)(2,1)} fusion(bf16[1536,3072]{1,0:T(8,128)(2,1)} %all-gather.5.cloned.1.call-done, bf16[1536,128]{1,0:T(8,128)(2,1)} %all_gather.22), kind=kOutput, calls=%fused_computation.23 | convolution fusion | flops 1208352768 | bytes 10616832 | tf_op jit(solution)/shard_map/dot_general | solution.py:29
  125.9 22.2 %all_gather.23 = bf16[3072,128]{1,0:T(8,128)(2,1)S(1)} all-gather(bf16[384,128]{1,0:T(8,128)(2,1)S(1)} %copy-done.3), channel_id=1, replica_groups=mesh['ia'=8,'ja'=8,'al'=8] {'ia'}, dimensions={0}, use_global_device_ids=true | all-gather | bytes 884736 | tf_op jit(solution)/shard_map/all_gather | solution.py:68
  148.0 51.2 %all-reduce.2.cloned.1.call-done = bf16[3072,128]{1,0:T(8,128)(2,1)} async-done(((bf16[3072,128]{1,0:T(8,128)(2,1)}), bf16[3072,128]{1,0:T(8,128)(2,1)}) %all-reduce.2.cloned.1.call-update) | async-done | bytes 786448 | tf_op jit(solution)/shard_map/psum | solution.py:70
  199.2 3.5 fusion.16
  203.5 24.1 %all_gather.25 = bf16[1536,128]{1,0:T(8,128)(2,1)S(1)} all-gather(bf16[192,128]{1,0:T(8,128)(2,1)S(1)} %copy-done.4), channel_id=1, replica_groups=mesh['ia'=8,'ja'=8,'al'=8] {'ja'}, dimensions={0}, use_global_device_ids=true | all-gather | bytes 442368 | tf_op jit(solution)/shard_map/all_gather | solution.py:62
  227.6 55.1 %all_to_all.32 = bf16[8,192,128]{2,1,0:T(8,128)(2,1)S(1)} all-to-all(bf16[8,192,128]{2,1,0:T(8,128)(2,1)S(1)} %bitcast.31), channel_id=1, replica_groups=mesh['ia'=8,'ja'=8,'al'=8] {'al'}, dimensions={0} | all-to-all | bytes 786432 | tf_op jit(solution)/shard_map/all_to_all | solution.py:83
  282.7 5.6 %all-to-all-start.1 = ((bf16[8,192,128]{2,1,0:T(8,128)(2,1)}), bf16[8,192,128]{2,1,0:T(8,128)(2,1)S(1)}, u32[]{:S(2)}, u32[]{:S(2)}) async-start(bf16[8,192,128]{2,1,0:T(8,128)(2,1)} %bitcast.8), calls=%async_computation.1 | async-start | bytes 786432 | tf_op jit(solution)/shard_map/all_to_all | solution.py:84
  288.7 31.5 %all-to-all-done.1 = bf16[8,192,128]{2,1,0:T(8,128)(2,1)S(1)} async-done(((bf16[8,192,128]{2,1,0:T(8,128)(2,1)}), bf16[8,192,128]{2,1,0:T(8,128)(2,1)S(1)}, u32[]{:S(2)}, u32[]{:S(2)}) %all-to-all-start.1) | async-done | bytes 393248 | tf_op jit(solution)/shard_map/all_to_all | solution.py:84
  320.6 5.2 all-gather.7.cloned.1.call-done
  325.9 6.9 %fusion.8 = bf16[1536,128]{0,1:T(8,128)(2,1)S(1)} fusion(bf16[3072,128]{1,0:T(8,128)(2,1)S(1)} %copy-done, bf16[1536,3072]{1,0:T(8,128)(2,1)} %all-gather.7.cloned.1.call-done), kind=kOutput, calls=%fused_computation.25 | convolution fusion | flops 1208156160 | bytes 10616832 | tf_op jit(solution)/shard_map/dot_general | solution.py:74
  333.8 67.9 %all-gather.9.cloned.1.call-done = bf16[3072,1024]{1,0:T(8,128)(2,1)} async-done(((bf16[3072,128]{1,0:T(8,128)(2,1)}), bf16[3072,1024]{1,0:T(8,128)(2,1)}) %all-gather.9.cloned.1.call-update) | async-done | bytes 6291472 | tf_op jit(solution)/shard_map/all_gather | solution.py:88
  401.8 44.1 %while.49 = (s32[]{:T(128)}, bf16[3,64,3072]{2,1,0:T(8,128)(2,1)S(1)}, bf16[3,64,1024]{2,1,0:T(8,128)(2,1)S(1)}, bf16[3072,1024]{1,0:T(8,128)(2,1)}, s32[]{:T(12...) while((s32[]{:T(128)}, bf16[3,64,3072]{2,1,0:T(8,128)(2,1)S(1)}, ...), condition=%wide.region_5.6_spmd, body=%wide.region_2.5_spmd.sunk | while | flops 51511300 | bytes 4605266 | solution.py:56
  401.9 14.6 %while.52 = (s32[]{:T(128)}, f32[64,3072]{1,0:T(8,128)S(1)}, bf16[64,1024]{1,0:T(8,128)(2,1)S(1)}, bf16[3072,1024]{1,0:T(8,128)(2,1)}, s32[]{:T(128)}, /*index=5*/s32[]{:T(128)}, s32[]{:T(128)}, s32[]{:T(128)}) while((s32[]{:T(128)}, f32[64,3072]{1,0:T(8,128)S(1)}, bf16[64,1024]{1,0:T(8,128)(2,1)S(1)}, ...), condition=%wide.region_4.4_spmd.clone, body=%wide.region_3.3_spmd.clone.sunk | while | flops 51314692 | bytes 3163285 | solution.py:53
  416.5 14.6 %while.52 = (s32[]{:T(128)}, f32[64,3072]{1,0:T(8,128)S(1)}, bf16[64,1024]{1,0:T(8,128)(2,1)S(1)}, bf16[3072,1024]{1,0:T(8,128)(2,1)}, s32[]{:T(128)}, /*index=5*/s32[]{:T(128)}, s32[]{:T(128)}, s32[]{:T(128)}) while((s32[]{:T(128)}, f32[64,3072]{1,0:T(8,128)S(1)}, bf16[64,1024]{1,0:T(8,128)(2,1)S(1)}, ...), condition=%wide.region_4.4_spmd.clone, body=%wide.region_3.3_spmd.clone.sunk | while | flops 51314692 | bytes 3163285 | solution.py:53
  416.6 1.6 fusion.35
  431.3 14.6 %while.52 = (s32[]{:T(128)}, f32[64,3072]{1,0:T(8,128)S(1)}, bf16[64,1024]{1,0:T(8,128)(2,1)S(1)}, bf16[3072,1024]{1,0:T(8,128)(2,1)}, s32[]{:T(128)}, /*index=5*/s32[]{:T(128)}, s32[]{:T(128)}, s32[]{:T(128)}) while((s32[]{:T(128)}, f32[64,3072]{1,0:T(8,128)S(1)}, bf16[64,1024]{1,0:T(8,128)(2,1)S(1)}, ...), condition=%wide.region_4.4_spmd.clone, body=%wide.region_3.3_spmd.clone.sunk | while | flops 51314692 | bytes 3163285 | solution.py:53
  440.4 1.6 fusion.35
  447.0 33.0 %all-gather.11.cloned.1.call-done = bf16[3072,1024]{1,0:T(8,128)(2,1)} async-done(((bf16[3072,128]{1,0:T(8,128)(2,1)}), bf16[3072,1024]{1,0:T(8,128)(2,1)}) %all-gather.11.cloned.1.call-update) | async-done | bytes 6291472 | tf_op jit(solution)/shard_map/all_gather | solution.py:87
  480.1 43.9 %while.51 = (s32[]{:T(128)}, bf16[3,64,3072]{2,1,0:T(8,128)(2,1)S(1)}, bf16[3,64,1024]{2,1,0:T(8,128)(2,1)S(1)}, bf16[3072,1024]{1,0:T(8,128)(2,1)}, s32[]{:T(12...) while((s32[]{:T(128)}, bf16[3,64,3072]{2,1,0:T(8,128)(2,1)S(1)}, ...), condition=%wide.region_9.10_spmd, body=%wide.region_6.9_spmd.sunk | while | flops 51511300 | bytes 4605266 | solution.py:56
  480.2 14.5 %while.53 = (s32[]{:T(128)}, f32[64,3072]{1,0:T(8,128)S(1)}, bf16[64,1024]{1,0:T(8,128)(2,1)S(1)}, bf16[3072,1024]{1,0:T(8,128)(2,1)}, s32[]{:T(128)}, /*index=5*/s32[]{:T(128)}, s32[]{:T(128)}, s32[]{:T(128)}) while((s32[]{:T(128)}, f32[64,3072]{1,0:T(8,128)S(1)}, bf16[64,1024]{1,0:T(8,128)(2,1)S(1)}, ...), condition=%wide.region_8.8_spmd.clone, body=%wide.region_7.7_spmd.clone.sunk | while | flops 51314692 | bytes 3163285 | solution.py:53
  494.8 14.5 %while.53 = (s32[]{:T(128)}, f32[64,3072]{1,0:T(8,128)S(1)}, bf16[64,1024]{1,0:T(8,128)(2,1)S(1)}, bf16[3072,1024]{1,0:T(8,128)(2,1)}, s32[]{:T(128)}, /*index=5*/s32[]{:T(128)}, s32[]{:T(128)}, s32[]{:T(128)}) while((s32[]{:T(128)}, f32[64,3072]{1,0:T(8,128)S(1)}, bf16[64,1024]{1,0:T(8,128)(2,1)S(1)}, ...), condition=%wide.region_8.8_spmd.clone, body=%wide.region_7.7_spmd.clone.sunk | while | flops 51314692 | bytes 3163285 | solution.py:53
  509.4 14.5 %while.53 = (s32[]{:T(128)}, f32[64,3072]{1,0:T(8,128)S(1)}, bf16[64,1024]{1,0:T(8,128)(2,1)S(1)}, bf16[3072,1024]{1,0:T(8,128)(2,1)}, s32[]{:T(128)}, /*index=5*/s32[]{:T(128)}, s32[]{:T(128)}, s32[]{:T(128)}) while((s32[]{:T(128)}, f32[64,3072]{1,0:T(8,128)S(1)}, bf16[64,1024]{1,0:T(8,128)(2,1)S(1)}, ...), condition=%wide.region_8.8_spmd.clone, body=%wide.region_7.7_spmd.clone.sunk | while | flops 51314692 | bytes 3163285 | solution.py:53
  (142 shorter events, 89.2 us)
Async XLA Ops:
  7.2 110.6 %all-gather.5.cloned.1.call-start = ((), (), s32[]{:S(2)}) async-start(), calls=%async_computation.3 | async-start | bytes 10616832 | tf_op jit(solution)/shard_map/all_gather | solution.py:69
  7.9 191.3 %all-reduce.2.cloned.1.call-start = ((), (), s32[]{:S(2)}) async-start(), calls=%async_computation.4 | async-start | bytes 1572864 | tf_op jit(solution)/shard_map/psum | solution.py:70
  125.0 0.9 copy-start.3
  125.0 200.9 %all-gather.7.cloned.1.call-start = ((), (), s32[]{:S(2)}) async-start(), calls=%async_computation.5 | async-start | bytes 10616832 | tf_op jit(solution)/shard_map/all_gather | solution.py:75
  125.7 276.0 %all-gather.9.cloned.1.call-start = ((), (), s32[]{:S(2)}) async-start(), calls=%async_computation.6 | async-start | bytes 7077888 | tf_op jit(solution)/shard_map/all_gather | solution.py:88
  202.7 0.8 copy-start.4
  202.8 277.3 %all-gather.11.cloned.1.call-start = ((), (), s32[]{:S(2)}) async-start(), calls=%async_computation.7 | async-start | bytes 7077888 | tf_op jit(solution)/shard_map/all_gather | solution.py:87
  282.7 37.5 %all-to-all-start.1 = ((bf16[8,192,128]{2,1,0:T(8,128)(2,1)}), bf16[8,192,128]{2,1,0:T(8,128)(2,1)S(1)}, u32[]{:S(2)}, u32[]{:S(2)}) async-start(bf16[8,192,128]{2,1,0:T(8,128)(2,1)} %bitcast.8), calls=%async_computation.1 | async-start | bytes 786432 | tf_op jit(solution)/shard_map/all_to_all | solution.py:84
  288.3 235.8 %reduce-scatter.4.cloned.1.call-start = ((), (), s32[]{:S(2)}) async-start(), calls=%async_computation.8 | async-start | bytes 442368
  288.3 37.6 %copy-start = (bf16[3072,128]{1,0:T(8,128)(2,1)S(1)}, bf16[3072,128]{1,0:T(8,128)(2,1)}, u32[]{:S(2)}) copy-start(bf16[3072,128]{1,0:T(8,128)(2,1)} %get-tuple-element.279) | copy-start | bytes 2359300
  446.0 1.0 copy-start.2
  524.0 1.0 copy-start.1
Sparse Core Ops, SparseCore 0:
  10.1 107.5 all-gather.4
  125.1 74.0 all-reduce.1
  201.6 124.2 all-gather.6
  328.6 73.0 all-gather.8
  404.5 75.4 all-gather.10
  483.5 35.2 reduce-scatter.3
where the time goes:
time: 534 us; the launch traced here: 532 us
  waiting for transfers between devices  274 us (51%)
  blocking collectives  128 us (24%)
  matrix products  87.8 us (16%)
  other arithmetic  15.8 us (3%)
  between operations  14.2 us (3%)
  starting transfers between devices  5.79 us (1%)
    all_gather x1, waiting for transfers between devices, shards(): lax.all_gather(w_down, 'al', axis=0, tiled=True)  82.8 us
    dot_general x48, matrix products, contract_last(): lax.dot_general(left, right, (((1,), (1,)), ((), ())), preferred_element_...  73.6 us
    all_gather x1, waiting for transfers between devices, shards(): lax.all_gather(hidden_grad, 'al', axis=1, tiled=True)  67.9 us
    all_to_all x1, blocking collectives, shards(): lax.all_to_all(tokens_full, 'al', split_axis=0, concat_axis=1, tiled=True)  55.1 us
    psum x1, waiting for transfers between devices, shards(): lax.psum(act_partial.astype(jnp.bfloat16), 'ia').astype(jnp.float32)  51.2 us
    all_gather x1, waiting for transfers between devices, shards(): lax.all_gather(act_full, 'al', axis=1, tiled=True)  33 us
    all_to_all x1, waiting for transfers between devices, shards(): lax.all_to_all(grads_full, 'al', split_axis=0, concat_axis=1, tiled=True)  31.5 us
    all_gather x1, blocking collectives, shards(): lax.all_gather(out_grad, 'ja', axis=0, tiled=True)  27 us
  transfers between devices with their start and end apart: 7, of which 6 were waited for; matrix products, arithmetic and copies ran while one was open for 19% of the time, Pallas kernels for 0%

commit v1 on v0

v1 whole, which is shorter than its diff:
```python
import functools
import math

import jax
import jax.numpy as jnp
from jax import lax
from jax.experimental import pallas as pl
from jax.experimental.pallas import tpu as pltpu
from jax.sharding import PartitionSpec as P

MESH = pl.DeviceIdType.MESH
BF16, F32 = jnp.bfloat16, jnp.float32
gelu_root = math.sqrt(2.0 / math.pi)
gelu_cubic = 0.044715

N = 8
Z = 4
TB = 128
FB = 384
M = 4
DB = 192
DC = 2 * DB
TH = Z * TB
RIGHT_HOPS = (4, 4, 3, 3)
Z_ORDER = (2, 1, 3, 0)


def gelu_parts(value):
    tangent = jnp.tanh(gelu_root * (value + gelu_cubic * value * value * value))
    active = 0.5 * value * (1.0 + tangent)
    slope = 0.5 * (1.0 + tangent) + 0.5 * value * (1.0 - tangent * tangent) * gelu_root * (
        1.0 + 3.0 * gelu_cubic * value * value
    )
    return active, slope


def hops(side, d):
    return RIGHT_HOPS[d] if side == 0 else N - 1 - RIGHT_HOPS[d]


def kernel(
    scale, x_ref, g_ref, pre_ref, wu_ref, wd_ref, ig_ref, du_ref, dd_ref,
    gbuf, xbuf, gt, wd_v, wu_v, p, rs, zrec, act, hg, pre_v, slope, part,
    stage_d, stage_u, qb, qt, qrec,
    loc_sem, pre_sem, g_ss, g_rs, x_ss, x_rs, tw_ss, tw_rs, w_ss, w_rs,
    a_zs, a_zr, a_ys, a_yr, r_zs, r_zr, r_ys, r_yr, h_zs, h_zr, h_ys, h_yr,
    o_ss, o_rs, q_ss, q_rs,
):
    i, j, a = lax.axis_index("ia"), lax.axis_index("ja"), lax.axis_index("al")
    zh, c = a // 2, a % 2
    par = i % 2
    own_rows = pl.ds(pl.multiple_of(c * DB, 64), DB)
    other_rows = pl.ds(pl.multiple_of((1 - c) * DB, 64), DB)
    twin = (i, j, a + 1 - 2 * c)
    y_to = ((lax.rem(i + 1, N), j, a), (lax.rem(i + N - 1, N), j, a))
    z_to = [(i, j, lax.rem(zh + d, Z) * 2 + c) for d in range(Z)]
    z_of = [lax.rem(zh + d, Z) for d in range(Z)]
    zsrc = [lax.rem(zh + Z - d, Z) for d in range(Z)]
    partner = (2 * (i // 2) + c, j, 2 * zh + par)
    spread = [(i, lax.rem(j + d, N), 2 * (j // 2) + c) for d in range(N)]
    collect = [(i, 2 * zh + e, 2 * zs + c) for e in range(2) for zs in range(Z)]
    home = j // 2 == zh
    pending = []

    def remote(src, dst, ss, rr, dev):
        return pltpu.make_async_remote_copy(
            src_ref=src, dst_ref=dst, send_sem=ss, recv_sem=rr, device_id=dev, device_id_type=MESH
        )

    def send(src, dst, ss, rr, dev):
        copy = remote(src, dst, ss, rr, dev)
        copy.start()
        pending.append(copy)

    def arrived(dst, ss, rr):
        remote(dst, dst, ss, rr, twin).wait_recv()

    def blk(buf, r, z):
        r = lax.rem(r + 2 * N, N)
        row = pl.multiple_of((r % 2) * TH + z * TB, TB)
        return buf.at[r // 2, pl.ds(row, TB), :]

    local = []
    for w_ref, w_v, s in ((wd_ref, wd_v, 0), (wu_ref, wu_v, 1)):
        for m in range(M):
            cols = pl.ds(pl.multiple_of((2 * m + c) * FB, 128), FB)
            cp = pltpu.make_async_copy(w_ref.at[:, cols], w_v.at[m, own_rows, :], loc_sem.at[s, m])
            cp.start()
            local.append(cp)

    barrier = pltpu.get_barrier_semaphore()

    def greet(dev):
        pl.semaphore_signal(barrier, inc=1, device_id=dev, device_id_type=MESH)

    for dev in (twin, y_to[0], y_to[1], z_to[1], z_to[2], z_to[3]):
        greet(dev)

    @pl.when(c != par)
    def _():
        greet(partner)

    for d in range(N):
        if d == 0:
            @pl.when(jnp.logical_not(home))
            def _():
                greet(spread[0])
        else:
            greet(spread[d])
    for dev in collect:
        @pl.when(jnp.logical_not((dev[1] == j) & (dev[2] == a)))
        def _():
            greet(dev)
    swap = jnp.where(c != par, 1, 0)
    both = jnp.where(home, 14, 16)
    pl.semaphore_wait(barrier, 6 + swap + both)

    def spread_start(src_ref, buf, ss, rr):
        row = pl.multiple_of((j % 2) * DB, 64)
        lane = pl.multiple_of(c * TH + zh * TB, TB)
        dst = buf.at[pl.ds(row, DB), pl.ds(lane, TB)]
        slot = (j % 2) * Z + zh

        @pl.when(home)
        def _():
            pltpu.make_async_copy(src_ref, dst, rr.at[slot]).start()

        @pl.when(jnp.logical_not(home))
        def _():
            remote(src_ref, dst, ss.at[0], rr.at[slot], spread[0]).start()

        for d in range(1, N):
            send(src_ref, dst, ss.at[d], rr.at[slot], spread[d])

    def spread_wait(src_ref, buf, ss, rr):
        for e in range(2):
            for zs in range(Z):
                lane = pl.multiple_of(c * TH + zs * TB, TB)
                arrived(buf.at[e * DB:(e + 1) * DB, pl.ds(lane, TB)], ss.at[0], rr.at[e * Z + zs])

    def spread_end(src_ref, buf, ss, rr):
        @pl.when(jnp.logical_not(home))
        def _():
            remote(src_ref, buf.at[0:DB, 0:TB], ss.at[0], rr.at[0], spread[0]).wait_send()

    own_half = pl.ds(pl.multiple_of(c * TH, TB), TH)
    other_half = pl.ds(pl.multiple_of((1 - c) * TH, TB), TH)

    spread_start(g_ref, gbuf, g_ss, g_rs)

    @pl.when(c == par)
    def _():
        pltpu.make_async_copy(pre_ref, pre_v, pre_sem.at[1]).start()

    @pl.when(c != par)
    def _():
        remote(pre_ref, pre_v, pre_sem.at[0], pre_sem.at[1], partner).start()

    def weights_to_twin(w_ref, w_v, s):
        for m in range(M):
            cols = pl.ds(pl.multiple_of((2 * m + 1 - c) * FB, 128), FB)
            send(w_ref.at[:, cols], w_v.at[m, own_rows, :], w_ss.at[s, m], w_rs.at[s, m], twin)

    def weights_wait(w_v, s):
        for m in range(M):
            local[s * M + m].wait()
            arrived(w_v.at[m, other_rows, :], w_ss.at[s, m], w_rs.at[s, m])

    weights_to_twin(wd_ref, wd_v, 0)

    arrived(pre_v, pre_sem.at[0], pre_sem.at[1])
    active, slope_now = gelu_parts(pre_v[...].astype(F32).T)
    blk(act, i, zh)[...] = active.astype(BF16)
    slope[...] = slope_now

    def ag_z(buf, zs, zr):
        for d in (2, 1, 3):
            send(blk(buf, i, zh), blk(buf, i, zh), zs.at[d], zr.at[d], z_to[d])

    def ag_z_wait(buf, zs, zr, d):
        arrived(blk(buf, i, zsrc[d]), zs.at[d], zr.at[d])

    def ag_send(buf, ys, yr, side, s, d):
        if s < hops(side, d):
            ref = blk(buf, i - s if side == 0 else i + s, zsrc[d])
            send(ref, ref, ys.at[side, s, d], yr.at[side, s, d], y_to[side])

    def ag_wait(buf, ys, yr, side, s, d):
        if s < hops(side, d):
            ref = blk(buf, i - s - 1 if side == 0 else i + s + 1, zsrc[d])
            arrived(ref, ys.at[side, s, d], yr.at[side, s, d])

    def ag_step(buf, ys, yr, s, ds=(0, 1, 3, 2)):
        for d in ds:
            for side in range(2):
                if s > 0:
                    ag_wait(buf, ys, yr, side, s - 1, d)
                ag_send(buf, ys, yr, side, s, d)

    ag_z(act, a_zs, a_zr)
    ag_step(act, a_ys, a_yr, 0, (0,))

    spread_wait(g_ref, gbuf, g_ss, g_rs)
    send(gbuf.at[:, own_half], gbuf.at[:, own_half], tw_ss.at[0], tw_rs.at[0], twin)

    def turn(tp):
        def one(z, carry):
            lane = pl.multiple_of(tp * TH + z * TB, TB)
            row = pl.multiple_of(z * TB, TB)
            gt[tp, pl.ds(row, TB), :] = gbuf[:, pl.ds(lane, TB)].T
            return carry
        lax.fori_loop(0, Z, one, 0)

    turn(c)
    spread_start(x_ref, xbuf, x_ss, x_rs)
    weights_to_twin(wu_ref, wu_v, 1)
    weights_wait(wd_v, 0)
    arrived(gbuf.at[:, other_half], tw_ss.at[0], tw_rs.at[0])
    turn(1 - c)

    def partial(r):
        r = lax.rem(r + 2 * N, N)
        row = pl.multiple_of((r % 2) * TH, TB)
        term = jnp.dot(gt[r % 2], wd_v[r // 2], preferred_element_type=F32)
        p[r // 2, pl.ds(row, TH), :] = term.astype(BF16)

    def rs_out(side, s, d):
        h = hops(side, d)
        return i + h - s if side == 0 else i - h + s

    def rs_send(side, s, d):
        src = blk(p, rs_out(side, s, d), z_of[d]) if s == 0 else rs.at[side, s - 1, d]
        send(src, rs.at[side, s, d], r_ys.at[side, s, d], r_yr.at[side, s, d], y_to[side])

    def rs_wait(side, s, d):
        arrived(rs.at[side, s, d], r_ys.at[side, s, d], r_yr.at[side, s, d])

    def rs_step(s):
        for d in Z_ORDER:
            for side in range(2):
                if s < hops(side, d) - 1:
                    rs_wait(side, s, d)
                    mine = blk(p, rs_out(side, s + 1, d), z_of[d])
                    got = rs.at[side, s, d]
                    got[...] = (got[...].astype(F32) + mine[...].astype(F32)).astype(BF16)
                    rs_send(side, s + 1, d)

    partial(i + 4)
    for d in Z_ORDER:
        rs_send(0 if hops(0, d) == 4 else 1, 0, d)
    partial(i + 3)
    partial(i - 3)
    for d in Z_ORDER:
        rs_send(1 if hops(0, d) == 4 else 0, 0, d)

    def rest(k, carry):
        partial(i + N - 2 + k)
        return carry
    lax.fori_loop(0, 5, rest, 0)

    ag_step(act, a_ys, a_yr, 1, (0,))
    for d in (1, 3, 2):
        ag_z_wait(act, a_zs, a_zr, d)
        ag_step(act, a_ys, a_yr, 0, (d,))
    rs_step(0)
    ag_step(act, a_ys, a_yr, 1, (1, 3, 2))
    spread_wait(x_ref, xbuf, x_ss, x_rs)
    send(xbuf.at[:, own_half], xbuf.at[:, own_half], tw_ss.at[1], tw_rs.at[1], twin)
    rs_step(1)
    ag_step(act, a_ys, a_yr, 2)
    rs_step(2)

    for d in Z_ORDER:
        total = blk(p, i, z_of[d])[...].astype(F32)
        for side in range(2):
            s = hops(side, d) - 1
            rs_wait(side, s, d)
            total = total + rs[side, s, d].astype(F32)
        if d == 0:
            part[...] = total
        else:
            out = rs.at[0, hops(0, d) - 1, d]
            out[...] = total.astype(BF16)
            send(out, zrec.at[d], r_zs.at[d], r_zr.at[d], z_to[d])
    ag_step(act, a_ys, a_yr, 3)
    total = part[...]
    for d in (1, 3, 2):
        arrived(zrec.at[d], r_zs.at[d], r_zr.at[d])
        total = total + zrec[d].astype(F32)
    blk(hg, i, zh)[...] = (total * slope[...]).astype(BF16)

    ag_z(hg, h_zs, h_zr)
    ag_step(hg, h_ys, h_yr, 0, (0,))

    def weight_grad(feat, hid, stage, m):
        term = jnp.dot(feat[...], hid[m], preferred_element_type=F32) * scale
        stage[m] = term.astype(BF16)

    outs = []

    def weight_out(stage, out_ref, s, m):
        cols = pl.ds(pl.multiple_of((2 * m + c) * FB, 128), FB)
        cp = pltpu.make_async_copy(stage.at[m, own_rows, :], out_ref.at[:, cols], loc_sem.at[2 + s, m])
        cp.start()
        outs.append(cp)
        send(stage.at[m, other_rows, :], out_ref.at[:, cols], o_ss.at[s, m], o_rs.at[s, m], twin)

    def weight_arrived(out_ref, s, m):
        cols = pl.ds(pl.multiple_of((2 * m + 1 - c) * FB, 128), FB)
        arrived(out_ref.at[:, cols], o_ss.at[s, m], o_rs.at[s, m])

    for d in range(Z):
        for side in range(2):
            ag_wait(act, a_ys, a_yr, side, 3, d)
    weight_grad(gbuf, act, stage_d, 0)
    weight_out(stage_d, dd_ref, 0, 0)
    ag_step(hg, h_ys, h_yr, 1, (0,))
    for d in (1, 3, 2):
        ag_z_wait(hg, h_zs, h_zr, d)
        ag_step(hg, h_ys, h_yr, 0, (d,))
    for m in (1, 2):
        weight_grad(gbuf, act, stage_d, m)
        weight_out(stage_d, dd_ref, 0, m)
    ag_step(hg, h_ys, h_yr, 2, (0,))
    ag_step(hg, h_ys, h_yr, 1, (1, 3, 2))
    weight_grad(gbuf, act, stage_d, 3)
    weight_out(stage_d, dd_ref, 0, 3)
    arrived(xbuf.at[:, other_half], tw_ss.at[1], tw_rs.at[1])
    weights_wait(wu_v, 1)
    ag_step(hg, h_ys, h_yr, 2, (1, 3, 2))
    ag_step(hg, h_ys, h_yr, 3)

    def input_part(tp):
        row = pl.multiple_of(tp * TH, TB)
        total = jnp.zeros((DC, TH), F32)
        for m in range(M):
            total = total + lax.dot_general(
                wu_v[m], hg[m, pl.ds(row, TH), :], (((1,), (1,)), ((), ())),
                preferred_element_type=F32,
            )
        qb[tp] = total.astype(BF16)

    early = 1 - par
    input_part(early)

    @pl.when(c != early)
    def _():
        remote(qb.at[early], qt, tw_ss.at[2], tw_rs.at[2], twin).start()

    for d in range(Z):
        for side in range(2):
            ag_wait(hg, h_ys, h_yr, side, 3, d)
    input_part(par)

    @pl.when(c != par)
    def _():
        remote(qb.at[par], qt, tw_ss.at[2], tw_rs.at[2], twin).start()

    weight_grad(xbuf, hg, stage_u, 0)
    weight_out(stage_u, du_ref, 1, 0)
    arrived(qt, tw_ss.at[2], tw_rs.at[2])
    qb[c] = (qb[c].astype(F32) + qt[...].astype(F32)).astype(BF16)
    for e in range(2):
        for zs in range(Z):
            dev = collect[e * Z + zs]
            mine = (dev[1] == j) & (dev[2] == a)
            src = qb.at[c, e * DB:(e + 1) * DB, zs * TB:(zs + 1) * TB]

            @pl.when(mine)
            def _():
                pltpu.make_async_copy(src, qrec.at[j], q_rs.at[j]).start()

            @pl.when(jnp.logical_not(mine))
            def _():
                remote(src, qrec.at[j], q_ss.at[e * Z + zs], q_rs.at[j], dev).start()

    for m in range(1, M):
        weight_grad(xbuf, hg, stage_u, m)
        weight_out(stage_u, du_ref, 1, m)

    total = jnp.zeros((DB, TB), F32)
    for d in range(N):
        arrived(qrec.at[d], q_ss.at[0], q_rs.at[d])
        total = total + qrec[d].astype(F32)
    ig_ref[...] = total.astype(BF16)

    for s, out_ref in ((0, dd_ref), (1, du_ref)):
        for m in range(M):
            weight_arrived(out_ref, s, m)
    for cp in outs:
        cp.wait()
    for copy in pending:
        copy.wait_send()
    spread_end(g_ref, gbuf, g_ss, g_rs)
    spread_end(x_ref, xbuf, x_ss, x_rs)

    @pl.when(c != par)
    def _():
        remote(pre_ref, pre_v, pre_sem.at[0], pre_sem.at[1], partner).wait_send()

    remote(qb.at[0], qt, tw_ss.at[2], tw_rs.at[2], twin).wait_send()
    for e in range(2):
        for zs in range(Z):
            dev = collect[e * Z + zs]
            src = qb.at[c, e * DB:(e + 1) * DB, zs * TB:(zs + 1) * TB]

            @pl.when(jnp.logical_not((dev[1] == j) & (dev[2] == a)))
            def _():
                remote(src, qrec.at[j], q_ss.at[e * Z + zs], q_rs.at[j], dev).wait_send()


def shards(inputs, out_grad, pre_act, w_up, w_down):
    scale = float(inputs.shape[1] * N) ** (-0.5)
    dma = pltpu.SemaphoreType.DMA
    any_spec = pl.BlockSpec(memory_space=pl.ANY)
    return pl.pallas_call(
        functools.partial(kernel, scale),
        out_shape=(
            jax.ShapeDtypeStruct((DB, TB), BF16),
            jax.ShapeDtypeStruct((DB, N * FB), BF16),
            jax.ShapeDtypeStruct((DB, N * FB), BF16),
        ),
        in_specs=[any_spec] * 5,
        out_specs=(pl.BlockSpec(memory_space=pltpu.VMEM), any_spec, any_spec),
        scratch_shapes=[
            pltpu.VMEM((DC, 2 * TH), BF16),
            pltpu.VMEM((DC, 2 * TH), BF16),
            pltpu.VMEM((2, TH, DC), BF16),
            pltpu.VMEM((M, DC, FB), BF16),
            pltpu.VMEM((M, DC, FB), BF16),
            pltpu.VMEM((M, 2 * TH, FB), BF16),
            pltpu.VMEM((2, 4, Z, TB, FB), BF16),
            pltpu.VMEM((Z, TB, FB), BF16),
            pltpu.VMEM((M, 2 * TH, FB), BF16),
            pltpu.VMEM((M, 2 * TH, FB), BF16),
            pltpu.VMEM((FB, TB), BF16),
            pltpu.VMEM((TB, FB), F32),
            pltpu.VMEM((TB, FB), F32),
            pltpu.VMEM((M, DC, FB), BF16),
            pltpu.VMEM((M, DC, FB), BF16),
            pltpu.VMEM((2, DC, TH), BF16),
            pltpu.VMEM((DC, TH), BF16),
            pltpu.VMEM((N, DB, TB), BF16),
            dma((4, M)), dma((2,)), dma((N,)), dma((N,)), dma((N,)), dma((N,)),
            dma((3,)), dma((3,)), dma((2, M)), dma((2, M)),
            dma((Z,)), dma((Z,)), dma((2, 4, Z)), dma((2, 4, Z)),
            dma((Z,)), dma((Z,)), dma((2, 4, Z)), dma((2, 4, Z)),
            dma((Z,)), dma((Z,)), dma((2, 4, Z)), dma((2, 4, Z)),
            dma((2, M)), dma((2, M)), dma((N,)), dma((N,)),
        ],
        compiler_params=pltpu.CompilerParams(
            collective_id=0, has_side_effects=True, vmem_limit_bytes=44 * 2**20
        ),
    )(inputs, out_grad, pre_act, w_up, w_down)


def solution(mesh):
    in_specs = (
        P(("ia", "ja"), "al"),
        P(("ia", "ja"), "al"),
        P(("ja", "ia"), "al"),
        P(("ia", "al"), "ja"),
        P(("ia", "al"), "ja"),
    )
    out_specs = (P(("ia", "ja"), "al"), P(("ia", "al"), "ja"), P(("ia", "al"), "ja"))
    return jax.shard_map(shards, mesh=mesh, in_specs=in_specs, out_specs=out_specs, check_vma=False)
```

time: 534 us -> 166 us (0.31)
  the two profiles are of different devices: /device:TPU:1 before, /device:TPU:75 now
where the time goes in v1:
time: 166 us
  Pallas kernels  158 us (95%)
  local copies, waits for them, and re-layouts  7.67 us (5%)
    pallas_call x1, Pallas kernels, shards(): pl.pallas_call(functools.partial(kernel, scale), out_shape=(jax.ShapeDtyp...  158 us
    unnamed x13, local copies, waits for them, and re-layouts  7.67 us

profile of v1, /device:TPU:75, one launch (start us, length us, event | category | flops | bytes accessed | tf_op | source)
XLA Modules:
  0.0 166.0 jit_solution(13986007810627505005)
XLA Ops:
  0.6 0.0 copy-start
  0.6 1.3 copy-done
  1.9 0.0 copy-start.1
  1.9 1.3 copy-done.1
  3.2 0.0 copy-start.2
  3.2 0.9 copy-done.2
  4.1 0.0 copy-start.3
  4.1 0.8 copy-done.3
  4.9 0.0 copy-start.4
  4.9 0.8 copy-done.4
  5.7 157.6 %shard_map.76 = (bf16[192,128]{1,0:T(8,128)(2,1)S(1)}, bf16[192,3072]{1,0:T(8,128)(2,1)S(1)}, bf16[192,3072]{1,0:T(8,128)(2,1)S(1)}) custom-call(bf16[192,128]{1,0:T(8,128)(2,1)S(1)} %copy-done.3, bf16[192,128]{1,0:T(8,128)(2,1)S(1)} %copy-done.4, bf16[384,128]{1,0:T(8,128)(2,1)S(1)} %copy-done.2, bf16[192,3072]{1,0:T(8,128)(2,1)S(1)} %copy-done, ...), custom_call_target="tpu_custom_call" | custom-call | tf_op jit(solution)/shard_map/pallas_call | solution.py:416
  163.3 0.6 copy.11
  163.9 1.0 copy.12
  164.9 1.0 copy.13
Async XLA Ops:
  0.6 1.3 copy-start
  1.9 1.3 copy-start.1
  3.2 0.9 copy-start.2
  4.1 0.8 copy-start.3
  4.9 0.8 copy-start.4

commit v2 on v1

--- a/solution.py
+++ b/solution.py
@@ -23,6 +23,8 @@
 TH = Z * TB
 RIGHT_HOPS = (4, 4, 3, 3)
 Z_ORDER = (2, 1, 3, 0)
+ACT_ROWS = 96
+HB = TB // 2
 
 
 def gelu_parts(value):
@@ -41,8 +43,8 @@
 def kernel(
     scale, x_ref, g_ref, pre_ref, wu_ref, wd_ref, ig_ref, du_ref, dd_ref,
     gbuf, xbuf, gt, wd_v, wu_v, p, rs, zrec, act, hg, pre_v, slope, part,
-    stage_d, stage_u, qb, qt, qrec,
-    loc_sem, pre_sem, g_ss, g_rs, x_ss, x_rs, tw_ss, tw_rs, w_ss, w_rs,
+    stage_d, stage_u, qb, qt, qrec, pre_own, act_own, qacc,
+    loc_sem, pre_sem, act_sem, a_bs, a_br, g_ss, g_rs, x_ss, x_rs, tw_ss, tw_rs, w_ss, w_rs,
     a_zs, a_zr, a_ys, a_yr, r_zs, r_zr, r_ys, r_yr, h_zs, h_zr, h_ys, h_yr,
     o_ss, o_rs, q_ss, q_rs,
 ):
@@ -75,10 +77,13 @@
     def arrived(dst, ss, rr):
         remote(dst, dst, ss, rr, twin).wait_recv()
 
-    def blk(buf, r, z):
+    def blk(buf, r, z, first=0, count=TB):
         r = lax.rem(r + 2 * N, N)
-        row = pl.multiple_of((r % 2) * TH + z * TB, TB)
-        return buf.at[r // 2, pl.ds(row, TB), :]
+        row = pl.multiple_of((r % 2) * TH + z * TB + first, 16)
+        return buf.at[r // 2, pl.ds(row, count), :]
+
+    pre_in = pltpu.make_async_copy(pre_ref, pre_own, pre_sem.at[2])
+    pre_in.start()
 
     local = []
     for w_ref, w_v, s in ((wd_ref, wd_v, 0), (wu_ref, wu_v, 1)):
@@ -113,6 +118,9 @@
             greet(dev)
     swap = jnp.where(c != par, 1, 0)
     both = jnp.where(home, 14, 16)
+
+    pre_in.wait()
+    act_own[...] = gelu_parts(pre_own[...].astype(F32).T)[0].astype(BF16)
     pl.semaphore_wait(barrier, 6 + swap + both)
 
     def spread_start(src_ref, buf, ss, rr):
@@ -148,13 +156,17 @@
 
     spread_start(g_ref, gbuf, g_ss, g_rs)
 
+    there = 2 * (i // 2) + c
+
     @pl.when(c == par)
     def _():
-        pltpu.make_async_copy(pre_ref, pre_v, pre_sem.at[1]).start()
+        pltpu.make_async_copy(act_own, blk(act, i, zh), act_sem.at[1]).start()
+        pltpu.make_async_copy(pre_own, pre_v, pre_sem.at[1]).start()
 
     @pl.when(c != par)
     def _():
-        remote(pre_ref, pre_v, pre_sem.at[0], pre_sem.at[1], partner).start()
+        remote(act_own, blk(act, there, zh), act_sem.at[0], act_sem.at[1], partner).start()
+        remote(pre_own, pre_v, pre_sem.at[0], pre_sem.at[1], partner).start()
 
     def weights_to_twin(w_ref, w_v, s):
         for m in range(M):
@@ -168,37 +180,79 @@
 
     weights_to_twin(wd_ref, wd_v, 0)
 
+    class Gather:
+        def __init__(self, buf, base, count, rows, sems):
+            self.buf, self.base, self.count, self.rows, self.sems = buf, base, count, rows, sems
+
+        def whole(self, r, z):
+            return blk(self.buf, r, z, self.base, self.count)
+
+        def first(self, r, z):
+            return blk(self.buf, r, z, self.base, self.rows)
+
+        def rest(self, r, z):
+            return blk(self.buf, r, z, self.base + self.rows, self.count - self.rows)
+
+        def z_start(self):
+            zs, zr = self.sems[:2]
+            for d in (2, 1, 3):
+                ref = self.whole(i, zh)
+                send(ref, ref, zs.at[d], zr.at[d], z_to[d])
+
+        def z_wait(self, d):
+            zs, zr = self.sems[:2]
+            arrived(self.whole(i, zsrc[d]), zs.at[d], zr.at[d])
+
+        def y_ref(self, r, d):
+            return self.first(r, zsrc[d]) if d else self.whole(r, zh)
+
+        def y_send(self, side, s, d):
+            ys, yr = self.sems[2:4]
+            if s < hops(side, d):
+                ref = self.y_ref(i - s if side == 0 else i + s, d)
+                send(ref, ref, ys.at[side, s, d], yr.at[side, s, d], y_to[side])
+
+        def y_wait(self, side, s, d):
+            ys, yr = self.sems[2:4]
+            if s < hops(side, d):
+                ref = self.y_ref(i - s - 1 if side == 0 else i + s + 1, d)
+                arrived(ref, ys.at[side, s, d], yr.at[side, s, d])
+
+        def b_send(self, side, s):
+            if s < hops(side, 0) and self.rows < self.count:
+                bs, br = self.sems[4:]
+                ref = self.rest(i - s - 1 if side == 0 else i + s + 1, zh)
+                for d in (2, 1, 3):
+                    send(ref, ref, bs.at[side, s, d], br.at[side, s, d], z_to[d])
+
+        def b_wait(self, s):
+            for side in range(2):
+                if s < hops(side, 0) and self.rows < self.count:
+                    bs, br = self.sems[4:]
+                    for d in (1, 3, 2):
+                        ref = self.rest(i - s - 1 if side == 0 else i + s + 1, zsrc[d])
+                        arrived(ref, bs.at[side, s, d], br.at[side, s, d])
+
+        def step(self, s, ds):
+            for d in ds:
+                for side in range(2):
+                    if s > 0:
+                        self.y_wait(side, s - 1, d)
+                    self.y_send(side, s, d)
+                    if s > 0 and d == 0:
+                        self.b_send(side, s - 1)
+
+    far = (1, 3, 2)
+    g_act = Gather(act, 0, TB, ACT_ROWS, (a_zs, a_zr, a_ys, a_yr, a_bs, a_br))
+    g_hid = [
+        Gather(hg, h * HB, HB, HB, (h_zs.at[h], h_zr.at[h], h_ys.at[h], h_yr.at[h])) for h in range(2)
+    ]
+
+    arrived(blk(act, i, zh), act_sem.at[0], act_sem.at[1])
+    g_act.step(0, (0,))
     arrived(pre_v, pre_sem.at[0], pre_sem.at[1])
-    active, slope_now = gelu_parts(pre_v[...].astype(F32).T)
-    blk(act, i, zh)[...] = active.astype(BF16)
-    slope[...] = slope_now
-
-    def ag_z(buf, zs, zr):
-        for d in (2, 1, 3):
-            send(blk(buf, i, zh), blk(buf, i, zh), zs.at[d], zr.at[d], z_to[d])
-
-    def ag_z_wait(buf, zs, zr, d):
-        arrived(blk(buf, i, zsrc[d]), zs.at[d], zr.at[d])
-
-    def ag_send(buf, ys, yr, side, s, d):
-        if s < hops(side, d):
-            ref = blk(buf, i - s if side == 0 else i + s, zsrc[d])
-            send(ref, ref, ys.at[side, s, d], yr.at[side, s, d], y_to[side])
-
-    def ag_wait(buf, ys, yr, side, s, d):
-        if s < hops(side, d):
-            ref = blk(buf, i - s - 1 if side == 0 else i + s + 1, zsrc[d])
-            arrived(ref, ys.at[side, s, d], yr.at[side, s, d])
-
-    def ag_step(buf, ys, yr, s, ds=(0, 1, 3, 2)):
-        for d in ds:
-            for side in range(2):
-                if s > 0:
-                    ag_wait(buf, ys, yr, side, s - 1, d)
-                ag_send(buf, ys, yr, side, s, d)
-
-    ag_z(act, a_zs, a_zr)
-    ag_step(act, a_ys, a_yr, 0, (0,))
+    slope[...] = gelu_parts(pre_v[...].astype(F32).T)[1]
+    g_act.step(1, (0,))
 
     spread_wait(g_ref, gbuf, g_ss, g_rs)
     send(gbuf.at[:, own_half], gbuf.at[:, own_half], tw_ss.at[0], tw_rs.at[0], twin)
@@ -212,8 +266,6 @@
         lax.fori_loop(0, Z, one, 0)
 
     turn(c)
-    spread_start(x_ref, xbuf, x_ss, x_rs)
-    weights_to_twin(wu_ref, wu_v, 1)
     weights_wait(wd_v, 0)
     arrived(gbuf.at[:, other_half], tw_ss.at[0], tw_rs.at[0])
     turn(1 - c)
@@ -228,69 +280,112 @@
         h = hops(side, d)
         return i + h - s if side == 0 else i - h + s
 
-    def rs_send(side, s, d):
-        src = blk(p, rs_out(side, s, d), z_of[d]) if s == 0 else rs.at[side, s - 1, d]
-        send(src, rs.at[side, s, d], r_ys.at[side, s, d], r_yr.at[side, s, d], y_to[side])
-
-    def rs_wait(side, s, d):
-        arrived(rs.at[side, s, d], r_ys.at[side, s, d], r_yr.at[side, s, d])
-
-    def rs_step(s):
+    def rs_at(h, side, s, d):
+        return rs.at[side, s, d, h * HB:(h + 1) * HB]
+
+    def p_at(h, r, d):
+        return blk(p, r, z_of[d], h * HB, HB)
+
+    def rs_send(h, side, s, d):
+        src = p_at(h, rs_out(side, s, d), d) if s == 0 else rs_at(h, side, s - 1, d)
+        send(src, rs_at(h, side, s, d), r_ys.at[h, side, s, d], r_yr.at[h, side, s, d], y_to[side])
+
+    def rs_wait(h, side, s, d):
+        arrived(rs_at(h, side, s, d), r_ys.at[h, side, s, d], r_yr.at[h, side, s, d])
+
+    def rs_start(h, long):
+        for d in Z_ORDER:
+            rs_send(h, 0 if (hops(0, d) == 4) == long else 1, 0, d)
+
+    def rs_step(h, s):
         for d in Z_ORDER:
             for side in range(2):
                 if s < hops(side, d) - 1:
-                    rs_wait(side, s, d)
-                    mine = blk(p, rs_out(side, s + 1, d), z_of[d])
-                    got = rs.at[side, s, d]
+                    rs_wait(h, side, s, d)
+                    mine = p_at(h, rs_out(side, s + 1, d), d)
+                    got = rs_at(h, side, s, d)
                     got[...] = (got[...].astype(F32) + mine[...].astype(F32)).astype(BF16)
-                    rs_send(side, s + 1, d)
+                    rs_send(h, side, s + 1, d)
+
+    def rs_end(h):
+        for d in Z_ORDER:
+            total = p_at(h, i, d)[...].astype(F32)
+            for side in range(2):
+                s = hops(side, d) - 1
+                rs_wait(h, side, s, d)
+                total = total + rs_at(h, side, s, d)[...].astype(F32)
+            if d == 0:
+                part[h * HB:(h + 1) * HB] = total
+            else:
+                out = rs_at(h, 0, hops(0, d) - 1, d)
+                out[...] = total.astype(BF16)
+                send(out, zrec.at[d, h * HB:(h + 1) * HB], r_zs.at[h, d], r_zr.at[h, d], z_to[d])
+
+    def hidden(h):
+        rows = slice(h * HB, (h + 1) * HB)
+        total = part[rows]
+        for d in far:
+            arrived(zrec.at[d, rows], r_zs.at[h, d], r_zr.at[h, d])
+            total = total + zrec[d, rows].astype(F32)
+        blk(hg, i, zh, h * HB, HB)[...] = (total * slope[rows]).astype(BF16)
+        g_hid[h].z_start()
+        g_hid[h].step(0, (0,))
+
+    def cross(gather):
+        for d in far:
+            gather.z_wait(d)
+            gather.step(0, (d,))
 
     partial(i + 4)
-    for d in Z_ORDER:
-        rs_send(0 if hops(0, d) == 4 else 1, 0, d)
+    rs_start(0, True)
     partial(i + 3)
     partial(i - 3)
-    for d in Z_ORDER:
-        rs_send(1 if hops(0, d) == 4 else 0, 0, d)
+    rs_start(0, False)
+    g_act.step(2, (0,))
 
     def rest(k, carry):
         partial(i + N - 2 + k)
         return carry
     lax.fori_loop(0, 5, rest, 0)
 
-    ag_step(act, a_ys, a_yr, 1, (0,))
-    for d in (1, 3, 2):
-        ag_z_wait(act, a_zs, a_zr, d)
-        ag_step(act, a_ys, a_yr, 0, (d,))
-    rs_step(0)
-    ag_step(act, a_ys, a_yr, 1, (1, 3, 2))
+    g_act.z_start()
+    rs_step(0, 0)
+    rs_step(0, 1)
+    g_act.step(3, (0,))
+    rs_step(0, 2)
+    rs_start(1, True)
+    rs_start(1, False)
+    weights_to_twin(wu_ref, wu_v, 1)
+    g_act.step(4, (0,))
+    rs_end(0)
+    rs_step(1, 0)
+    rs_step(1, 1)
+    hidden(0)
+    rs_step(1, 2)
+    g_hid[0].step(1, (0,))
+    cross(g_hid[0])
+    rs_end(1)
+    g_hid[0].step(2, (0,))
+    g_hid[0].step(1, far)
+    hidden(1)
+    g_hid[0].step(3, (0,))
+    g_hid[0].step(2, far)
+    g_hid[1].step(1, (0,))
+    cross(g_hid[1])
+    spread_start(x_ref, xbuf, x_ss, x_rs)
+    cross(g_act)
+    g_hid[0].step(3, far)
+    g_hid[1].step(2, (0,))
+    g_hid[1].step(1, far)
+    g_hid[0].step(4, (0,) + far)
+    g_act.step(1, far)
+    g_hid[1].step(3, (0,))
+    g_hid[1].step(2, far)
+    g_act.step(2, far)
+    g_hid[1].step(3, far)
     spread_wait(x_ref, xbuf, x_ss, x_rs)
     send(xbuf.at[:, own_half], xbuf.at[:, own_half], tw_ss.at[1], tw_rs.at[1], twin)
-    rs_step(1)
-    ag_step(act, a_ys, a_yr, 2)
-    rs_step(2)
-
-    for d in Z_ORDER:
-        total = blk(p, i, z_of[d])[...].astype(F32)
-        for side in range(2):
-            s = hops(side, d) - 1
-            rs_wait(side, s, d)
-            total = total + rs[side, s, d].astype(F32)
-        if d == 0:
-            part[...] = total
-        else:
-            out = rs.at[0, hops(0, d) - 1, d]
-            out[...] = total.astype(BF16)
-            send(out, zrec.at[d], r_zs.at[d], r_zr.at[d], z_to[d])
-    ag_step(act, a_ys, a_yr, 3)
-    total = part[...]
-    for d in (1, 3, 2):
-        arrived(zrec.at[d], r_zs.at[d], r_zr.at[d])
-        total = total + zrec[d].astype(F32)
-    blk(hg, i, zh)[...] = (total * slope[...]).astype(BF16)
-
-    ag_z(hg, h_zs, h_zr)
-    ag_step(hg, h_ys, h_yr, 0, (0,))
+    weights_wait(wu_v, 1)
 
     def weight_grad(feat, hid, stage, m):
         term = jnp.dot(feat[...], hid[m], preferred_element_type=F32) * scale
@@ -309,74 +404,66 @@
         cols = pl.ds(pl.multiple_of((2 * m + 1 - c) * FB, 128), FB)
         arrived(out_ref.at[:, cols], o_ss.at[s, m], o_rs.at[s, m])
 
-    for d in range(Z):
-        for side in range(2):
-            ag_wait(act, a_ys, a_yr, side, 3, d)
-    weight_grad(gbuf, act, stage_d, 0)
-    weight_out(stage_d, dd_ref, 0, 0)
-    ag_step(hg, h_ys, h_yr, 1, (0,))
-    for d in (1, 3, 2):
-        ag_z_wait(hg, h_zs, h_zr, d)
-        ag_step(hg, h_ys, h_yr, 0, (d,))
-    for m in (1, 2):
+    early = 1 - par
+    last = lax.rem(i + 4, N) // 2
+
+    def input_part(tp, m):
+        row = pl.multiple_of(tp * TH, TB)
+        return lax.dot_general(
+            wu_v[m], hg[m, pl.ds(row, TH), :], (((1,), (1,)), ((), ())),
+            preferred_element_type=F32,
+        )
+
+    def input_to_twin(tp):
+        @pl.when(c != tp)
+        def _():
+            remote(qb.at[tp], qt, tw_ss.at[2], tw_rs.at[2], twin).start()
+
+    def input_out(tp):
+        @pl.when(c == tp)
+        def _():
+            arrived(qt, tw_ss.at[2], tw_rs.at[2])
+            qb[c] = (qb[c].astype(F32) + qt[...].astype(F32)).astype(BF16)
+            for e in range(2):
+                for zs in range(Z):
+                    dev = collect[e * Z + zs]
+                    mine = (dev[1] == j) & (dev[2] == a)
+                    src = qb.at[c, e * DB:(e + 1) * DB, zs * TB:(zs + 1) * TB]
+
+                    @pl.when(mine)
+                    def _():
+                        pltpu.make_async_copy(src, qrec.at[j], q_rs.at[j]).start()
+
+                    @pl.when(jnp.logical_not(mine))
+                    def _():
+                        remote(src, qrec.at[j], q_ss.at[e * Z + zs], q_rs.at[j], dev).start()
+
+    qacc[...] = input_part(early, 0)
+    for m in range(1, M):
+        qacc[...] += input_part(early, m)
+    qb[early] = qacc[...].astype(BF16)
+    input_to_twin(early)
+    qacc[...] = input_part(par, lax.rem(last + 1, M))
+    for m in (2, 3):
+        qacc[...] += input_part(par, lax.rem(last + m, M))
+    input_out(early)
+    arrived(xbuf.at[:, other_half], tw_ss.at[1], tw_rs.at[1])
+    for m in (1, 2, 3):
+        weight_grad(xbuf, hg, stage_u, lax.rem(last + m, M))
+        weight_out(stage_u, du_ref, 1, lax.rem(last + m, M))
+    g_hid[1].step(4, (0,) + far)
+    qb[par] = (qacc[...] + input_part(par, last)).astype(BF16)
+    input_to_twin(par)
+    g_act.step(3, far)
+    weight_grad(xbuf, hg, stage_u, last)
+    weight_out(stage_u, du_ref, 1, last)
+    input_out(par)
+    for step in range(4):
+        g_act.b_wait(step)
+    g_act.step(4, far)
+    for m in range(M):
         weight_grad(gbuf, act, stage_d, m)
         weight_out(stage_d, dd_ref, 0, m)
-    ag_step(hg, h_ys, h_yr, 2, (0,))
-    ag_step(hg, h_ys, h_yr, 1, (1, 3, 2))
-    weight_grad(gbuf, act, stage_d, 3)
-    weight_out(stage_d, dd_ref, 0, 3)
-    arrived(xbuf.at[:, other_half], tw_ss.at[1], tw_rs.at[1])
-    weights_wait(wu_v, 1)
-    ag_step(hg, h_ys, h_yr, 2, (1, 3, 2))
-    ag_step(hg, h_ys, h_yr, 3)
-
-    def input_part(tp):
-        row = pl.multiple_of(tp * TH, TB)
-        total = jnp.zeros((DC, TH), F32)
-        for m in range(M):
-            total = total + lax.dot_general(
-                wu_v[m], hg[m, pl.ds(row, TH), :], (((1,), (1,)), ((), ())),
-                preferred_element_type=F32,
-            )
-        qb[tp] = total.astype(BF16)
-
-    early = 1 - par
-    input_part(early)
-
-    @pl.when(c != early)
-    def _():
-        remote(qb.at[early], qt, tw_ss.at[2], tw_rs.at[2], twin).start()
-
-    for d in range(Z):
-        for side in range(2):
-            ag_wait(hg, h_ys, h_yr, side, 3, d)
-    input_part(par)
-
-    @pl.when(c != par)
-    def _():
-        remote(qb.at[par], qt, tw_ss.at[2], tw_rs.at[2], twin).start()
-
-    weight_grad(xbuf, hg, stage_u, 0)
-    weight_out(stage_u, du_ref, 1, 0)
-    arrived(qt, tw_ss.at[2], tw_rs.at[2])
-    qb[c] = (qb[c].astype(F32) + qt[...].astype(F32)).astype(BF16)
-    for e in range(2):
-        for zs in range(Z):
-            dev = collect[e * Z + zs]
-            mine = (dev[1] == j) & (dev[2] == a)
-            src = qb.at[c, e * DB:(e + 1) * DB, zs * TB:(zs + 1) * TB]
-
-            @pl.when(mine)
-            def _():
-                pltpu.make_async_copy(src, qrec.at[j], q_rs.at[j]).start()
-
-            @pl.when(jnp.logical_not(mine))
-            def _():
-                remote(src, qrec.at[j], q_ss.at[e * Z + zs], q_rs.at[j], dev).start()
-
-    for m in range(1, M):
-        weight_grad(xbuf, hg, stage_u, m)
-        weight_out(stage_u, du_ref, 1, m)
 
     total = jnp.zeros((DB, TB), F32)
     for d in range(N):
@@ -396,7 +483,8 @@
 
     @pl.when(c != par)
     def _():
-        remote(pre_ref, pre_v, pre_sem.at[0], pre_sem.at[1], partner).wait_send()
+        remote(act_own, blk(act, there, zh), act_sem.at[0], act_sem.at[1], partner).wait_send()
+        remote(pre_own, pre_v, pre_sem.at[0], pre_sem.at[1], partner).wait_send()
 
     remote(qb.at[0], qt, tw_ss.at[2], tw_rs.at[2], twin).wait_send()
     for e in range(2):
@@ -441,15 +529,19 @@
             pltpu.VMEM((2, DC, TH), BF16),
             pltpu.VMEM((DC, TH), BF16),
             pltpu.VMEM((N, DB, TB), BF16),
-            dma((4, M)), dma((2,)), dma((N,)), dma((N,)), dma((N,)), dma((N,)),
+            pltpu.VMEM((FB, TB), BF16),
+            pltpu.VMEM((TB, FB), BF16),
+            pltpu.VMEM((DC, TH), F32),
+            dma((4, M)), dma((3,)), dma((2,)), dma((2, 4, Z)), dma((2, 4, Z)),
+             dma((N,)), dma((N,)), dma((N,)), dma((N,)),
             dma((3,)), dma((3,)), dma((2, M)), dma((2, M)),
             dma((Z,)), dma((Z,)), dma((2, 4, Z)), dma((2, 4, Z)),
-            dma((Z,)), dma((Z,)), dma((2, 4, Z)), dma((2, 4, Z)),
-            dma((Z,)), dma((Z,)), dma((2, 4, Z)), dma((2, 4, Z)),
+            dma((2, Z)), dma((2, Z)), dma((2, 2, 4, Z)), dma((2, 2, 4, Z)),
+            dma((2, Z)), dma((2, Z)), dma((2, 2, 4, Z)), dma((2, 2, 4, Z)),
             dma((2, M)), dma((2, M)), dma((N,)), dma((N,)),
         ],
         compiler_params=pltpu.CompilerParams(
-            collective_id=0, has_side_effects=True, vmem_limit_bytes=44 * 2**20
+            collective_id=0, has_side_effects=True, vmem_limit_bytes=60 * 2**20
         ),
     )(inputs, out_grad, pre_act, w_up, w_down)
 

time: 166 us -> 141 us (0.85)
  the two profiles are of different devices: /device:TPU:75 before, /device:TPU:66 now
where the time goes in v2:
time: 141 us; the launch traced here: 140 us
  Pallas kernels  135 us (96%)
  local copies, waits for them, and re-layouts  4.89 us (3%)
    pallas_call x1, Pallas kernels, shards(): pl.pallas_call(functools.partial(kernel, scale), out_shape=(jax.ShapeDtyp...  135 us
    unnamed x5, local copies, waits for them, and re-layouts  4.89 us

profile of v2, /device:TPU:66, one launch (start us, length us, event | category | flops | bytes accessed | tf_op | source)
XLA Modules:
  0.0 140.4 jit_solution(9359884273644020964)
XLA Ops:
  0.6 134.9 %shard_map.76 = (bf16[192,128]{1,0:T(8,128)(2,1)}, bf16[192,3072]{1,0:T(8,128)(2,1)}, bf16[192,3072]{1,0:T(8,128)(2,1)}) custom-call(bf16[192,128]{1,0:T(8,128)(2,1)} %x_ref.1, bf16[192,128]{1,0:T(8,128)(2,1)} %g_ref.1, bf16[384,128]{1,0:T(8,128)(2,1)} %pre_ref.1, bf16[192,3072]{1,0:T(8,128)(2,1)} %wu_ref.1, bf16[192,3072]{1,0:T(8,128)(2,1)} %wd_ref.1), custom_call_target="tpu_custom_call" | custom-call | tf_op jit(solution)/shard_map/pallas_call | solution.py:504
  135.5 1.4 %copy.11 = bf16[192,128]{1,0:T(8,128)(2,1)} copy(bf16[192,128]{1,0:T(8,128)(2,1)} %get-tuple-element.6) | data formatting | bytes 98304
  136.9 0.0 copy-start
  136.9 2.5 %copy.12 = bf16[192,3072]{1,0:T(8,128)(2,1)} copy(bf16[192,3072]{1,0:T(8,128)(2,1)} %get-tuple-element.7) | data formatting | bytes 2359296
  139.4 0.0 copy-done
  139.4 1.0 copy.13
Async XLA Ops:
  136.9 2.5 %copy-start = (bf16[192,3072]{1,0:T(8,128)(2,1)S(1)}, bf16[192,3072]{1,0:T(8,128)(2,1)}, u32[]{:S(2)}) copy-start(bf16[192,3072]{1,0:T(8,128)(2,1)} %get-tuple-element.8) | copy-start | bytes 3538948

commit v3 on v2

--- a/solution.py
+++ b/solution.py
@@ -140,19 +140,23 @@
         for d in range(1, N):
             send(src_ref, dst, ss.at[d], rr.at[slot], spread[d])
 
-    def spread_wait(src_ref, buf, ss, rr):
+    def spread_wait(buf, ss, rr, zs):
         for e in range(2):
-            for zs in range(Z):
-                lane = pl.multiple_of(c * TH + zs * TB, TB)
-                arrived(buf.at[e * DB:(e + 1) * DB, pl.ds(lane, TB)], ss.at[0], rr.at[e * Z + zs])
+            lane = pl.multiple_of(c * TH + zs * TB, TB)
+            arrived(buf.at[e * DB:(e + 1) * DB, pl.ds(lane, TB)], ss.at[0], rr.at[e * Z + zs])
+
+    def to_twin(buf, s, zs):
+        ref = buf.at[:, pl.ds(pl.multiple_of(c * TH + zs * TB, TB), TB)]
+        send(ref, ref, tw_ss.at[s, zs], tw_rs.at[s, zs], twin)
+
+    def from_twin(buf, s, zs):
+        ref = buf.at[:, pl.ds(pl.multiple_of((1 - c) * TH + zs * TB, TB), TB)]
+        arrived(ref, tw_ss.at[s, zs], tw_rs.at[s, zs])
 
     def spread_end(src_ref, buf, ss, rr):
         @pl.when(jnp.logical_not(home))
         def _():
             remote(src_ref, buf.at[0:DB, 0:TB], ss.at[0], rr.at[0], spread[0]).wait_send()
-
-    own_half = pl.ds(pl.multiple_of(c * TH, TB), TH)
-    other_half = pl.ds(pl.multiple_of((1 - c) * TH, TB), TH)
 
     spread_start(g_ref, gbuf, g_ss, g_rs)
 
@@ -239,8 +243,11 @@
                     if s > 0:
                         self.y_wait(side, s - 1, d)
                     self.y_send(side, s, d)
-                    if s > 0 and d == 0:
-                        self.b_send(side, s - 1)
+
+        def low(self, steps):
+            for s in steps:
+                for side in range(2):
+                    self.b_send(side, s)
 
     far = (1, 3, 2)
     g_act = Gather(act, 0, TB, ACT_ROWS, (a_zs, a_zr, a_ys, a_yr, a_bs, a_br))
@@ -254,21 +261,18 @@
     slope[...] = gelu_parts(pre_v[...].astype(F32).T)[1]
     g_act.step(1, (0,))
 
-    spread_wait(g_ref, gbuf, g_ss, g_rs)
-    send(gbuf.at[:, own_half], gbuf.at[:, own_half], tw_ss.at[0], tw_rs.at[0], twin)
-
-    def turn(tp):
-        def one(z, carry):
-            lane = pl.multiple_of(tp * TH + z * TB, TB)
-            row = pl.multiple_of(z * TB, TB)
-            gt[tp, pl.ds(row, TB), :] = gbuf[:, pl.ds(lane, TB)].T
-            return carry
-        lax.fori_loop(0, Z, one, 0)
-
-    turn(c)
+    def turn(tp, zs):
+        lane = pl.multiple_of(tp * TH + zs * TB, TB)
+        gt[tp, zs * TB:(zs + 1) * TB, :] = gbuf[:, pl.ds(lane, TB)].T
+
+    for zs in range(Z):
+        spread_wait(gbuf, g_ss, g_rs, zs)
+        to_twin(gbuf, 0, zs)
+        turn(c, zs)
     weights_wait(wd_v, 0)
-    arrived(gbuf.at[:, other_half], tw_ss.at[0], tw_rs.at[0])
-    turn(1 - c)
+    for zs in range(Z):
+        from_twin(gbuf, 0, zs)
+        turn(1 - c, zs)
 
     def partial(r):
         r = lax.rem(r + 2 * N, N)
@@ -351,6 +355,7 @@
     g_act.z_start()
     rs_step(0, 0)
     rs_step(0, 1)
+    g_act.low((0, 1))
     g_act.step(3, (0,))
     rs_step(0, 2)
     rs_start(1, True)
@@ -372,19 +377,17 @@
     g_hid[0].step(2, far)
     g_hid[1].step(1, (0,))
     cross(g_hid[1])
+    g_act.low((2, 3))
     spread_start(x_ref, xbuf, x_ss, x_rs)
-    cross(g_act)
     g_hid[0].step(3, far)
     g_hid[1].step(2, (0,))
     g_hid[1].step(1, far)
+    cross(g_act)
     g_hid[0].step(4, (0,) + far)
-    g_act.step(1, far)
     g_hid[1].step(3, (0,))
     g_hid[1].step(2, far)
-    g_act.step(2, far)
     g_hid[1].step(3, far)
-    spread_wait(x_ref, xbuf, x_ss, x_rs)
-    send(xbuf.at[:, own_half], xbuf.at[:, own_half], tw_ss.at[1], tw_rs.at[1], twin)
+    g_act.step(1, far)
     weights_wait(wu_v, 1)
 
     def weight_grad(feat, hid, stage, m):
@@ -414,21 +417,25 @@
             preferred_element_type=F32,
         )
 
-    def input_to_twin(tp):
+    def input_done(tp, zs, total):
+        qb[tp, :, zs * TB:(zs + 1) * TB] = total.astype(BF16)
+
         @pl.when(c != tp)
         def _():
-            remote(qb.at[tp], qt, tw_ss.at[2], tw_rs.at[2], twin).start()
+            cols = slice(zs * TB, (zs + 1) * TB)
+            remote(qb.at[tp, :, cols], qt.at[:, cols], tw_ss.at[2, zs], tw_rs.at[2, zs], twin).start()
 
     def input_out(tp):
         @pl.when(c == tp)
         def _():
-            arrived(qt, tw_ss.at[2], tw_rs.at[2])
-            qb[c] = (qb[c].astype(F32) + qt[...].astype(F32)).astype(BF16)
-            for e in range(2):
-                for zs in range(Z):
+            for zs in range(Z):
+                cols = slice(zs * TB, (zs + 1) * TB)
+                arrived(qt.at[:, cols], tw_ss.at[2, zs], tw_rs.at[2, zs])
+                qb[c, :, cols] = (qb[c, :, cols].astype(F32) + qt[:, cols].astype(F32)).astype(BF16)
+                for e in range(2):
                     dev = collect[e * Z + zs]
                     mine = (dev[1] == j) & (dev[2] == a)
-                    src = qb.at[c, e * DB:(e + 1) * DB, zs * TB:(zs + 1) * TB]
+                    src = qb.at[c, e * DB:(e + 1) * DB, cols]
 
                     @pl.when(mine)
                     def _():
@@ -441,29 +448,41 @@
     qacc[...] = input_part(early, 0)
     for m in range(1, M):
         qacc[...] += input_part(early, m)
-    qb[early] = qacc[...].astype(BF16)
-    input_to_twin(early)
+    for zs in range(Z):
+        input_done(early, zs, qacc[:, zs * TB:(zs + 1) * TB])
     qacc[...] = input_part(par, lax.rem(last + 1, M))
     for m in (2, 3):
         qacc[...] += input_part(par, lax.rem(last + m, M))
     input_out(early)
-    arrived(xbuf.at[:, other_half], tw_ss.at[1], tw_rs.at[1])
+    for zs in range(Z):
+        spread_wait(xbuf, x_ss, x_rs, zs)
+        to_twin(xbuf, 1, zs)
+    g_hid[1].step(4, (0,) + far)
+    for zs in range(Z):
+        row = pl.multiple_of(par * TH + zs * TB, TB)
+        term = lax.dot_general(
+            wu_v[last], hg[last, pl.ds(row, TB), :], (((1,), (1,)), ((), ())),
+            preferred_element_type=F32,
+        )
+        input_done(par, zs, qacc[:, zs * TB:(zs + 1) * TB] + term)
+    g_act.step(2, far)
+    input_out(par)
+    for zs in range(Z):
+        from_twin(xbuf, 1, zs)
     for m in (1, 2, 3):
         weight_grad(xbuf, hg, stage_u, lax.rem(last + m, M))
         weight_out(stage_u, du_ref, 1, lax.rem(last + m, M))
-    g_hid[1].step(4, (0,) + far)
-    qb[par] = (qacc[...] + input_part(par, last)).astype(BF16)
-    input_to_twin(par)
-    g_act.step(3, far)
     weight_grad(xbuf, hg, stage_u, last)
     weight_out(stage_u, du_ref, 1, last)
-    input_out(par)
+    g_act.step(3, far)
     for step in range(4):
         g_act.b_wait(step)
+    for m in (1, 2, 3):
+        weight_grad(gbuf, act, stage_d, lax.rem(last + m, M))
+        weight_out(stage_d, dd_ref, 0, lax.rem(last + m, M))
     g_act.step(4, far)
-    for m in range(M):
-        weight_grad(gbuf, act, stage_d, m)
-        weight_out(stage_d, dd_ref, 0, m)
+    weight_grad(gbuf, act, stage_d, last)
+    weight_out(stage_d, dd_ref, 0, last)
 
     total = jnp.zeros((DB, TB), F32)
     for d in range(N):
@@ -486,7 +505,9 @@
         remote(act_own, blk(act, there, zh), act_sem.at[0], act_sem.at[1], partner).wait_send()
         remote(pre_own, pre_v, pre_sem.at[0], pre_sem.at[1], partner).wait_send()
 
-    remote(qb.at[0], qt, tw_ss.at[2], tw_rs.at[2], twin).wait_send()
+    for zs in range(Z):
+        cols = slice(zs * TB, (zs + 1) * TB)
+        remote(qb.at[0, :, cols], qt.at[:, cols], tw_ss.at[2, zs], tw_rs.at[2, zs], twin).wait_send()
     for e in range(2):
         for zs in range(Z):
             dev = collect[e * Z + zs]
@@ -497,11 +518,28 @@
                 remote(src, qrec.at[j], q_ss.at[e * Z + zs], q_rs.at[j], dev).wait_send()
 
 
+def hand_over(ig_in, du_in, dd_in, ig_out, du_out, dd_out, ig_v, du_v, dd_v, in_sem, out_sem):
+    parts = [(ig_in, ig_v, ig_out)]
+    for src, mid, dst in ((du_in, du_v, du_out), (dd_in, dd_v, dd_out)):
+        for part in range(4):
+            rows = pl.ds(part * (DB // 4), DB // 4)
+            parts.append((src.at[rows, :], mid.at[rows, :], dst.at[rows, :]))
+    loads = [pltpu.make_async_copy(src, mid, in_sem.at[n]) for n, (src, mid, _) in enumerate(parts)]
+    stores = [pltpu.make_async_copy(mid, dst, out_sem.at[n]) for n, (_, mid, dst) in enumerate(parts)]
+    for load in loads:
+        load.start()
+    for load, store in zip(loads, stores):
+        load.wait()
+        store.start()
+    for store in stores:
+        store.wait()
+
+
 def shards(inputs, out_grad, pre_act, w_up, w_down):
     scale = float(inputs.shape[1] * N) ** (-0.5)
     dma = pltpu.SemaphoreType.DMA
     any_spec = pl.BlockSpec(memory_space=pl.ANY)
-    return pl.pallas_call(
+    results = pl.pallas_call(
         functools.partial(kernel, scale),
         out_shape=(
             jax.ShapeDtypeStruct((DB, TB), BF16),
@@ -534,7 +572,7 @@
             pltpu.VMEM((DC, TH), F32),
             dma((4, M)), dma((3,)), dma((2,)), dma((2, 4, Z)), dma((2, 4, Z)),
              dma((N,)), dma((N,)), dma((N,)), dma((N,)),
-            dma((3,)), dma((3,)), dma((2, M)), dma((2, M)),
+            dma((3, Z)), dma((3, Z)), dma((2, M)), dma((2, M)),
             dma((Z,)), dma((Z,)), dma((2, 4, Z)), dma((2, 4, Z)),
             dma((2, Z)), dma((2, Z)), dma((2, 2, 4, Z)), dma((2, 2, 4, Z)),
             dma((2, Z)), dma((2, Z)), dma((2, 2, 4, Z)), dma((2, 2, 4, Z)),
@@ -544,6 +582,14 @@
             collective_id=0, has_side_effects=True, vmem_limit_bytes=60 * 2**20
         ),
     )(inputs, out_grad, pre_act, w_up, w_down)
+    return pl.pallas_call(
+        hand_over,
+        out_shape=[jax.ShapeDtypeStruct(value.shape, value.dtype) for value in results],
+        in_specs=[any_spec] * 3,
+        out_specs=[any_spec] * 3,
+        scratch_shapes=[pltpu.VMEM(value.shape, value.dtype) for value in results] + [dma((9,)), dma((9,))],
+        compiler_params=pltpu.CompilerParams(vmem_limit_bytes=60 * 2**20),
+    )(*results)
 
 
 def solution(mesh):

time: 141 us -> 132 us (0.936)
  the two profiles are of different devices: /device:TPU:66 before, /device:TPU:1 now
where the time goes in v3:
time: 132 us; the launch traced here: 131 us
  Pallas kernels  131 us (99%)
    pallas_call x1, Pallas kernels, shards(): pl.pallas_call(functools.partial(kernel, scale), out_shape=(jax.ShapeDtyp...  128 us

profile of v3, /device:TPU:1, one launch (start us, length us, event | category | flops | bytes accessed | tf_op | source)
XLA Modules:
  0.0 131.4 jit_solution(10597317893832477397)
XLA Ops:
  0.6 128.2 %shard_map.76 = (bf16[192,128]{1,0:T(8,128)(2,1)}, bf16[192,3072]{1,0:T(8,128)(2,1)}, bf16[192,3072]{1,0:T(8,128)(2,1)}) custom-call(bf16[192,128]{1,0:T(8,128)(2,1)} %x_ref.1, bf16[192,128]{1,0:T(8,128)(2,1)} %g_ref.1, bf16[384,128]{1,0:T(8,128)(2,1)} %pre_ref.1, bf16[192,3072]{1,0:T(8,128)(2,1)} %wu_ref.1, bf16[192,3072]{1,0:T(8,128)(2,1)} %wd_ref.1), custom_call_target="tpu_custom_call" | custom-call | tf_op jit(solution)/shard_map/pallas_call | solution.py:542
  128.9 2.5 %shard_map.77 = (bf16[192,128]{1,0:T(8,128)(2,1)}, bf16[192,3072]{1,0:T(8,128)(2,1)}, bf16[192,3072]{1,0:T(8,128)(2,1)}) custom-call(bf16[192,128]{1,0:T(8,128)(2,1)} %get-tuple-element.6.ig_in, bf16[192,3072]{1,0:T(8,128)(2,1)} %get-tuple-element.7.du_in, bf16[192,3072]{1,0:T(8,128)(2,1)} %get-tuple-element.8.dd_in), custom_call_target="tpu_custom_call" | custom-call | tf_op jit(solution)/shard_map/pallas_call | solution.py:585

commit v4 on v3

--- a/solution.py
+++ b/solution.py
@@ -270,10 +270,6 @@
         to_twin(gbuf, 0, zs)
         turn(c, zs)
     weights_wait(wd_v, 0)
-    for zs in range(Z):
-        from_twin(gbuf, 0, zs)
-        turn(1 - c, zs)
-
     def partial(r):
         r = lax.rem(r + 2 * N, N)
         row = pl.multiple_of((r % 2) * TH, TB)
@@ -340,20 +336,27 @@
             gather.z_wait(d)
             gather.step(0, (d,))
 
-    partial(i + 4)
+    def own_tokens(k, carry):
+        partial(c + 2 * k)
+        return carry
+    lax.fori_loop(0, M, own_tokens, 0)
+
+    for zs in range(Z):
+        from_twin(gbuf, 0, zs)
+        turn(1 - c, zs)
+
+    def pick(mine, other):
+        return jnp.where(c == par, mine, other)
+
+    partial(pick(i + 3, i + 4))
+    partial(pick(i - 3, i + 2))
     rs_start(0, True)
-    partial(i + 3)
-    partial(i - 3)
     rs_start(0, False)
+    partial(pick(i + 1, i - 2))
+    partial(pick(i - 1, i))
+    rs_step(0, 0)
     g_act.step(2, (0,))
-
-    def rest(k, carry):
-        partial(i + N - 2 + k)
-        return carry
-    lax.fori_loop(0, 5, rest, 0)
-
     g_act.z_start()
-    rs_step(0, 0)
     rs_step(0, 1)
     g_act.low((0, 1))
     g_act.step(3, (0,))
@@ -382,8 +385,8 @@
     g_hid[0].step(3, far)
     g_hid[1].step(2, (0,))
     g_hid[1].step(1, far)
+    g_hid[0].step(4, (0,) + far)
     cross(g_act)
-    g_hid[0].step(4, (0,) + far)
     g_hid[1].step(3, (0,))
     g_hid[1].step(2, far)
     g_hid[1].step(3, far)

time: 132 us -> 133 us (level)
  no operation moved by 1% of the time
where the time goes in v4:
time: 133 us
  Pallas kernels  132 us (99%)
    pallas_call x1, Pallas kernels, shards(): pl.pallas_call(functools.partial(kernel, scale), out_shape=(jax.ShapeDtyp...  129 us

profile of v4, /device:TPU:1, one launch (start us, length us, event | category | flops | bytes accessed | tf_op | source)
XLA Modules:
  0.0 132.7 jit_solution(1150863187264714928)
XLA Ops:
  0.6 129.5 %shard_map.76 = (bf16[192,128]{1,0:T(8,128)(2,1)}, bf16[192,3072]{1,0:T(8,128)(2,1)}, bf16[192,3072]{1,0:T(8,128)(2,1)}) custom-call(bf16[192,128]{1,0:T(8,128)(2,1)} %x_ref.1, bf16[192,128]{1,0:T(8,128)(2,1)} %g_ref.1, bf16[384,128]{1,0:T(8,128)(2,1)} %pre_ref.1, bf16[192,3072]{1,0:T(8,128)(2,1)} %wu_ref.1, bf16[192,3072]{1,0:T(8,128)(2,1)} %wd_ref.1), custom_call_target="tpu_custom_call" | custom-call | tf_op jit(solution)/shard_map/pallas_call | solution.py:545
  130.1 2.5 %shard_map.77 = (bf16[192,128]{1,0:T(8,128)(2,1)}, bf16[192,3072]{1,0:T(8,128)(2,1)}, bf16[192,3072]{1,0:T(8,128)(2,1)}) custom-call(bf16[192,128]{1,0:T(8,128)(2,1)} %get-tuple-element.6.ig_in, bf16[192,3072]{1,0:T(8,128)(2,1)} %get-tuple-element.7.du_in, bf16[192,3072]{1,0:T(8,128)(2,1)} %get-tuple-element.8.dd_in), custom_call_target="tpu_custom_call" | custom-call | tf_op jit(solution)/shard_map/pallas_call | solution.py:588
